TPU v7x, 256 devices: a whole 4x4x8 slice. The times are simulated.
256 devices in a mesh: mic: 8 (over x, y_lo), grid: 32 (over y_hi, z, core).
Axes of the slice: x: 4, y: 4 (y_hi: 2, y_lo: 2; y = y_hi * 2 + y_lo), z: 8, core: 2. Of those that a mesh axis runs over, the one named last changes fastest.
Arguments:
- samples: bfloat16 [32, 4096, 4096], P('grid', 'mic'), may hold values from -6 to 6
- mic_places: float32 [3, 4096], P(None, 'mic'), may hold values from -0.5 to 0.5
- grid_places: float32 [3, 16384], P(None, 'grid'), may hold values from -0.5 to 0.5
Outputs:
- beam_map: float32 [16384], P('grid')
All inputs are finite; a program needn't handle non-finite values.
Results may differ from a plain program's by a relative error of at most 0.0077.
Values may be sent and summed in bfloat16 or wider, within the bound.
A program may use at most 64 MiB of HBM per device.

v0:
```python
import jax
import jax.numpy as jnp
from jax import lax
from jax.sharding import PartitionSpec as P

L = 4096
BIN = 512


WAVENUMBER = 120.0


def dft_table():
    steps = jnp.arange(L, dtype=jnp.int32)
    window = 0.5 - 0.5 * jnp.cos(2.0 * jnp.pi * steps.astype(jnp.float32) / L)
    scale = jnp.sqrt(jnp.sum(window * window))
    theta = 2.0 * jnp.pi * (BIN * steps % L).astype(jnp.float32) / L
    table = jnp.stack([window * jnp.cos(theta) / scale, -window * jnp.sin(theta) / scale], axis=1)
    return table.astype(jnp.bfloat16)


def steering(grid_block, mic_block):
    delta_x = grid_block[0][:, None] - mic_block[0][None, :]
    delta_y = grid_block[1][:, None] - mic_block[1][None, :]
    delta_z = grid_block[2][:, None] + 1.5 - mic_block[2][None, :]
    phase = WAVENUMBER * jnp.sqrt(delta_x * delta_x + delta_y * delta_y + delta_z * delta_z)
    return (jnp.cos(phase).astype(jnp.bfloat16), jnp.sin(phase).astype(jnp.bfloat16))


def contract_last(left, right):
    return lax.dot_general(
        left, right, (((1,), (1,)), ((), ())), preferred_element_type=jnp.float32
    )


def steer_block(spec_real, spec_imag, cos_part, sin_part):
    beam_real = contract_last(spec_real, cos_part) - contract_last(spec_imag, sin_part)
    beam_imag = contract_last(spec_imag, cos_part) + contract_last(spec_real, sin_part)
    return (beam_real, beam_imag)


def per_device(samples, mic_places, grid_places):
    table = dft_table()
    seg_local, mic_local, length = samples.shape
    flat = jnp.dot(samples.reshape(-1, length), table, preferred_element_type=jnp.float32)
    local_spec = jnp.moveaxis(flat.reshape(seg_local, mic_local, 2), 2, 0).astype(jnp.bfloat16)
    spectra = lax.all_gather(local_spec, "grid", axis=1, tiled=True)
    seg_total = spectra.shape[1]
    cycle_size = lax.axis_size("mic")
    mic_total = mic_local * cycle_size
    spec_real = spectra[0]
    spec_imag = spectra[1]
    real_f = spec_real.astype(jnp.float32)
    imag_f = spec_imag.astype(jnp.float32)
    power = jnp.sum(real_f * real_f + imag_f * imag_f)
    own_cos, own_sin = steering(grid_places, mic_places)
    own_real, own_imag = steer_block(spec_real, spec_imag, own_cos, own_sin)
    beam_real, beam_imag, power_all = lax.psum((own_real, own_imag, power), "mic")
    beam_map = (jnp.sum(beam_real * beam_real + beam_imag * beam_imag, axis=0) - power_all) / (
        seg_total * mic_total
    )
    return beam_map


def solution(mesh):
    in_specs = (P("grid", "mic", None), P(None, "mic"), P(None, "grid"))
    out_specs = P("grid")
    return jax.shard_map(
        per_device, mesh=mesh, in_specs=in_specs, out_specs=out_specs, check_vma=False
    )
```

profile of v0, /device:TPU:32, one launch (start us, length us, event | category | flops | bytes accessed | tf_op | source)
XLA Modules:
  0.0 158.7 jit_solution(11436409571731483518)
XLA Ops:
  6.5 0.0 all-reduce.3.cloned.1.call-start
  6.5 0.7 multiply_reduce_fusion
  7.9 0.8 fusion.27
  8.7 0.8 fusion.26
  9.5 1.0 divide_convert_fusion
  10.5 3.4 %fusion.5 = bf16[2,1,512]{2,0,1:T(2,128)(2,1)S(1)} fusion(bf16[1,512,4096]{2,1,0:T(8,128)(2,1)} %param.3, bf16[4096,1]{0,1:T(2,128)(2,1)S(1)} %get-tuple-element.15, bf16[4096,1]{0,1:T(2,128)(2,1)S(1)} %get-tuple-element.16), kind=kOutput, calls=%fused_computation.5 | convolution fusion | flops 8422400 | bytes 4212736 | tf_op jit(solution)/shard_map/dot_general | solution.py:45
  13.9 40.7 %all_gather.3 = bf16[2,32,512]{2,0,1:T(2,128)(2,1)S(1)} all-gather(bf16[2,1,512]{2,0,1:T(2,128)(2,1)S(1)} %fusion.5), channel_id=1, replica_groups=mesh['mic'=8,'grid'=32] {'grid'}, dimensions={1}, use_global_device_ids=true | all-gather | bytes 67584 | tf_op jit(solution)/shard_map/all_gather | solution.py:47
  54.6 0.1 fusion.25
  54.7 4.2 %fusion.9 = f32[32,512]{1,0:T(8,128)S(1)} fusion(f32[512]{0:T(512)S(1)} %bitcast.35, f32[512]{0:T(512)S(1)} %bitcast.47, f32[512]{0:T(512)S(1)} %bitcast.39, f32[512]{0:T(512)S(1)} %bitcast.51, f32[512]{0:T(512)S(1)} %bitcast.31, f32[512]{0:T(512)S(1)} %bitcast.43, bf16[1,32,512]{2,0,1:T(2,128)(2,1)S(1)} %get-tuple-element.7), kind=kOutput, calls=%fused_computation.10 | convolution fusion | flops 19398656 | bytes 110592 | tf_op jit(solution)/shard_map/dot_general | solution.py:31
  58.8 4.2 %fusion.8 = f32[32,512]{1,0:T(8,128)S(1)} fusion(f32[512]{0:T(512)S(1)} %bitcast.36, f32[512]{0:T(512)S(1)} %bitcast.48, f32[512]{0:T(512)S(1)} %bitcast.40, f32[512]{0:T(512)S(1)} %bitcast.52, f32[512]{0:T(512)S(1)} %bitcast.32, f32[512]{0:T(512)S(1)} %bitcast.44, bf16[1,32,512]{2,0,1:T(2,128)(2,1)S(1)} %get-tuple-element.8), kind=kOutput, calls=%fused_computation.9 | convolution fusion | flops 19398656 | bytes 110592 | tf_op jit(solution)/shard_map/dot_general | solution.py:31
  63.0 5.1 %convolution_subtract_fusion = f32[32,512]{1,0:T(8,128)} fusion(f32[32,512]{1,0:T(8,128)S(1)} %fusion.9, f32[512]{0:T(512)S(1)} %bitcast.37, f32[512]{0:T(512)S(1)} %bitcast.49, f32[512]{0:T(512)S(1)} %bitcast.41, f32[512]{0:T(512)S(1)} %bitcast.53, f32[512]{0:T(512)S(1)} %bitcast.33, f32[512]{0:T(512)S(1)} %bitcast.45, ...), kind=kOutput, calls=%fused_computation.3 | convolution fusion | flops 19415040 | bytes 176128 | tf_op jit(solution)/shard_map/dot_general | solution.py:31
  68.1 4.8 %convolution_add_fusion = f32[32,512]{1,0:T(8,128)} fusion(f32[32,512]{1,0:T(8,128)S(1)} %fusion.8, f32[512]{0:T(512)S(1)} %bitcast.38, f32[512]{0:T(512)S(1)} %bitcast.50, f32[512]{0:T(512)S(1)} %bitcast.42, f32[512]{0:T(512)S(1)} %bitcast.54, f32[512]{0:T(512)S(1)} %bitcast.34, f32[512]{0:T(512)S(1)} %bitcast.46, bf16[1,32,512]{2,0,1:T(2,128)(2,1)S(1)} %get-tuple-element.7), kind=kOutput, calls=%fused_computation.2 | convolution fusion | flops 19415040 | bytes 176128 | tf_op jit(solution)/shard_map/dot_general | solution.py:31
  72.9 0.0 all-reduce.3.cloned.1.call-update
  72.9 0.6 add_reduce_fusion
  73.5 19.5 %psum.23 = f32[]{:T(128)} all-reduce(f32[]{:T(128)} %add_reduce_fusion), channel_id=1, replica_groups=mesh['mic'=8,'grid'=32] {'mic'}, use_global_device_ids=true, to_apply=%region_5.6 | all-reduce | flops 1 | bytes 8 | tf_op jit(solution)/shard_map/psum | solution.py:58
  93.0 56.8 %all-reduce.3.cloned.1.call-done = (f32[32,512]{1,0:T(8,128)}, f32[32,512]{1,0:T(8,128)}) async-done(((f32[32,512]{1,0:T(8,128)}, f32[32,512]{1,0:T(8,128)}), (f32[32,512]{1,0:T(8,128)}, f32[32,512]{1,0:T(8,128)})) %all-reduce.3.cloned.1.call-update) | async-done | bytes 131088 | tf_op jit(solution)/shard_map/psum | solution.py:58
  149.8 0.9 add_reduce_fusion.1
  150.7 1.2 subtract_multiply_fusion
Async XLA Ops:
  6.5 143.3 %all-reduce.3.cloned.1.call-start = ((), (), s32[]{:S(2)}) async-start(), calls=%async_computation | async-start | bytes 262144 | tf_op jit(solution)/shard_map/psum | solution.py:58
Sparse Core Ops, SparseCore 0:
  73.0 76.7 all-reduce.2
where the time goes:
time: 159 us
  blocking collectives  60.2 us (38%)
  waiting for transfers between devices  56.8 us (36%)
  matrix products  21.6 us (14%)
  between operations  14.1 us (9%)
  other arithmetic  5.2 us (3%)
    psum x1, waiting for transfers between devices, per_device(): lax.psum((own_real, own_imag, power), 'mic')  56.8 us
    all_gather x1, blocking collectives, per_device(): spectra = lax.all_gather(local_spec, 'grid', axis=1, tiled=True)  40.7 us
    psum x1, blocking collectives, per_device(): lax.psum((own_real, own_imag, power), 'mic')  19.5 us
    dot_general x4, matrix products, contract_last(): lax.dot_general(left, right, (((1,), (1,)), ((), ())), preferred_element_...  18.2 us
    dot_general x1, matrix products, per_device(): jnp.dot(samples.reshape(-1, length), table, preferred_element_type=jnp.fl...  3.37 us
  transfers between devices with their start and end apart: 1, of which 1 were waited for; matrix products, arithmetic and copies ran while one was open for 0% of the time, Pallas kernels for 0%

commit v1 on v0

v1 whole, which is shorter than its diff:
```python
import jax
import jax.numpy as jnp
import ml_dtypes
import numpy as np
from jax import lax
from jax.experimental import pallas as pl
from jax.experimental.pallas import tpu as pltpu
from jax.sharding import PartitionSpec as P

L = 4096
BIN = 512
WAVENUMBER = 120.0
MESH = pl.DeviceIdType.MESH

NMIC = 8
NGRID = 32
NZ = 8
PARTS = 8
BATCHES = 4
SEGS = NGRID // BATCHES
TILES = 4


def dft_table():
    steps = np.arange(L, dtype=np.int64)
    window = (0.5 - 0.5 * np.cos(2.0 * np.pi * steps / L)).astype(np.float32)
    scale = np.sqrt(np.sum(window.astype(np.float64) ** 2)).astype(np.float32)
    theta = 2.0 * np.pi * ((BIN * steps) % L) / L
    real = window * np.cos(theta).astype(np.float32) / scale
    imag = -window * np.sin(theta).astype(np.float32) / scale
    rows = [real if (r % 8) < 4 else imag for r in range(16)]
    return np.stack(rows).astype(ml_dtypes.bfloat16)


def sine_cosine(turns):
    r = turns - jnp.round(turns)
    u = r * r
    s = SIN[-1]
    for coefficient in SIN[-2::-1]:
        s = s * u + coefficient
    s = s * r
    c = COS[-1]
    for coefficient in COS[-2::-1]:
        c = c * u + coefficient
    return s * c, 1.0 - s * s


def fitted():
    nodes = 0.125 - 0.125 * np.cos(np.pi * (np.arange(400) + 0.5) / 400)
    r = np.sqrt(nodes)
    sin_fit = np.polynomial.chebyshev.Chebyshev.fit(nodes, np.sqrt(2) * np.sin(np.pi * r) / r, 4, domain=[0, 0.25])
    cos_fit = np.polynomial.chebyshev.Chebyshev.fit(nodes, np.sqrt(2) * np.cos(np.pi * r), 4, domain=[0, 0.25])
    as_list = lambda fit: [float(v) for v in fit.convert(kind=np.polynomial.Polynomial).coef]
    return as_list(sin_fit), as_list(cos_fit)


SIN, COS = fitted()


def slot_of(grid):
    return (grid // 2 % NZ) * 4 + (grid // 16) * 2 + grid % 2


def grid_of(slot):
    return (slot // 2 % 2) * 16 + (slot // 4) * 2 + slot % 2


def kernel(
    samples, table_hbm, mic_hbm, grid_hbm, out_ref,
    parts, table, mic, grid, mic_columns, gather, unpacked, weights, beams,
    load_sem, small_sem, gsend, grecv, bsend, brecv,
):
    me_mic = lax.axis_index("mic")
    me_grid = lax.axis_index("grid")
    me = slot_of(me_grid)
    width = L // PARTS

    smalls = [
        pltpu.make_async_copy(src, dst, small_sem.at[i])
        for i, (src, dst) in enumerate([(table_hbm, table), (mic_hbm, mic), (grid_hbm, grid)])
    ]
    loads = [
        pltpu.make_async_copy(
            samples.at[0, :, pl.ds(p * width, width)], parts.at[p], load_sem.at[p]
        )
        for p in range(PARTS)
    ]
    smalls[0].start()
    for load in loads:
        load.start()
    smalls[1].start()
    smalls[2].start()

    barrier = pltpu.get_barrier_semaphore()

    def grid_peer(k):
        return lax.rem(me + k, NGRID)

    def mic_peer(k):
        return lax.rem(me_mic + k, NMIC)

    for k in range(1, NGRID):
        pl.semaphore_signal(
            barrier, inc=1, device_id=(me_mic, grid_of(grid_peer(k))), device_id_type=MESH
        )
    for k in range(1, NMIC):
        pl.semaphore_signal(
            barrier, inc=1, device_id=(mic_peer(k), me_grid), device_id_type=MESH
        )

    smalls[0].wait()
    total = jnp.zeros((16, 512), jnp.float32)
    for p in range(PARTS):
        loads[p].wait()
        total += lax.dot_general(
            table[:, p * width : (p + 1) * width],
            parts[p],
            (((1,), (1,)), ((), ())),
            preferred_element_type=jnp.float32,
        )
    total = total[:8]
    lane_block = lax.rem(lax.broadcasted_iota(jnp.int32, (8, 128), 0), 4)
    own = total[:, :128]
    for k in range(1, 4):
        own = jnp.where(lane_block == k, total[:, 128 * k : 128 * (k + 1)], own)
    gather[me] = own.astype(jnp.bfloat16)

    pl.semaphore_wait(barrier, NGRID + NMIC - 2)

    gather_copies = []
    for k in range(1, NGRID):
        copy = pltpu.make_async_remote_copy(
            src_ref=gather.at[me],
            dst_ref=gather.at[me],
            send_sem=gsend.at[k],
            recv_sem=grecv.at[me],
            device_id=(me_mic, grid_of(grid_peer(k))),
            device_id_type=MESH,
        )
        copy.start()
        gather_copies.append(copy)

    smalls[1].wait()
    smalls[2].wait()
    mic_columns[...] = jnp.concatenate(
        [mic[...], jnp.zeros((5, 512), jnp.float32)], axis=0
    ).T
    gx = grid[0:1, :]
    gy = grid[1:2, :]
    gz = grid[2:3, :] + 1.5
    rows = 32

    def steer(i, carry):
        at = pl.multiple_of(i * rows, rows)
        dx = gx - mic_columns[pl.ds(at, rows), 0:1]
        dy = gy - mic_columns[pl.ds(at, rows), 1:2]
        dz = gz - mic_columns[pl.ds(at, rows), 2:3]
        dist = jnp.sqrt(dx * dx + dy * dy + dz * dz)
        sine, cosine = sine_cosine(dist * (WAVENUMBER / (2.0 * np.pi)))
        weights[pl.ds(at, rows), :] = cosine.astype(jnp.bfloat16)
        weights[pl.ds(pl.multiple_of(at + 512, rows), rows), :] = sine.astype(jnp.bfloat16)
        return carry

    lax.fori_loop(0, 512 // rows, steer, 0)

    power = jnp.zeros((8, 128), jnp.float32)
    beam_copies = []
    for b in range(BATCHES):
        for s in range(b * SEGS, (b + 1) * SEGS):
            @pl.when(me != s)
            def _():
                pltpu.make_async_remote_copy(
                    src_ref=gather.at[s],
                    dst_ref=gather.at[s],
                    send_sem=gsend.at[0],
                    recv_sem=grecv.at[s],
                    device_id=(me_mic, me_grid),
                    device_id_type=MESH,
                ).wait_recv()
        block = gather[b * SEGS : (b + 1) * SEGS].astype(jnp.float32)
        power += jnp.sum(block * block, axis=0)
        unpacked[...] = block
        real = jnp.concatenate([unpacked[:, k, :] for k in range(4)], axis=1)
        imag = jnp.concatenate([unpacked[:, 4 + k, :] for k in range(4)], axis=1)
        left = jnp.concatenate(
            [
                jnp.concatenate([real, -imag], axis=1),
                jnp.concatenate([imag, real], axis=1),
            ],
            axis=0,
        ).astype(jnp.bfloat16)
        beam = jnp.dot(left, weights[...], preferred_element_type=jnp.float32)
        for q in range(4):
            beams[b, me_mic, q] = beam[:, 128 * q : 128 * (q + 1)].astype(jnp.bfloat16)
        tiles = TILES
        if b == BATCHES - 1:
            high = power.astype(jnp.bfloat16)
            low = (power - high.astype(jnp.float32)).astype(jnp.bfloat16)
            beams[b, me_mic, TILES] = jnp.concatenate([high, low], axis=0)
            tiles = TILES + 1
        for k in range(1, NMIC):
            copy = pltpu.make_async_remote_copy(
                src_ref=beams.at[b, me_mic, pl.ds(0, tiles)],
                dst_ref=beams.at[b, me_mic, pl.ds(0, tiles)],
                send_sem=bsend.at[b, k],
                recv_sem=brecv.at[b, me_mic],
                device_id=(mic_peer(k), me_grid),
                device_id_type=MESH,
            )
            copy.start()
            beam_copies.append(copy)

    sums = [jnp.zeros((8, 128), jnp.float32) for _ in range(4)]
    for b in range(BATCHES):
        tiles = TILES + 1 if b == BATCHES - 1 else TILES
        for j in range(NMIC):
            @pl.when(me_mic != j)
            def _():
                pltpu.make_async_remote_copy(
                    src_ref=beams.at[b, j, pl.ds(0, tiles)],
                    dst_ref=beams.at[b, j, pl.ds(0, tiles)],
                    send_sem=bsend.at[b, 0],
                    recv_sem=brecv.at[b, j],
                    device_id=(me_mic, me_grid),
                    device_id_type=MESH,
                ).wait_recv()
        for q in range(4):
            whole = beams[b, 0, q].astype(jnp.float32)
            for j in range(1, NMIC):
                whole += beams[b, j, q].astype(jnp.float32)
            whole = whole * whole
            sums[q] += whole[:8] + whole[8:]
    all_power = jnp.zeros((16, 128), jnp.float32)
    for j in range(NMIC):
        all_power += beams[BATCHES - 1, j, TILES].astype(jnp.float32)
    all_power = jnp.sum(all_power)
    for q in range(4):
        line = (jnp.sum(sums[q], axis=0) - all_power) * (1.0 / (NGRID * 512 * NMIC))
        out_ref[pl.ds(128 * q, 128)] = line

    for copy in gather_copies + beam_copies:
        copy.wait_send()


def per_device(samples, mic_places, grid_places):
    hbm = pl.BlockSpec(memory_space=pltpu.HBM)
    width = L // PARTS
    table = jnp.asarray(dft_table())
    return pl.pallas_call(
        kernel,
        out_shape=jax.ShapeDtypeStruct((512,), jnp.float32),
        in_specs=[hbm] * 4,
        out_specs=pl.BlockSpec(memory_space=pltpu.VMEM),
        scratch_shapes=[
            pltpu.VMEM((PARTS, 512, width), jnp.bfloat16),
            pltpu.VMEM((16, L), jnp.bfloat16),
            pltpu.VMEM((3, 512), jnp.float32),
            pltpu.VMEM((3, 512), jnp.float32),
            pltpu.VMEM((512, 8), jnp.float32),
            pltpu.VMEM((NGRID, 8, 128), jnp.bfloat16),
            pltpu.VMEM((SEGS, 8, 128), jnp.float32),
            pltpu.VMEM((1024, 512), jnp.bfloat16),
            pltpu.VMEM((BATCHES, NMIC, TILES + 1, 16, 128), jnp.bfloat16),
            pltpu.SemaphoreType.DMA((PARTS,)),
            pltpu.SemaphoreType.DMA((3,)),
            pltpu.SemaphoreType.DMA((NGRID,)),
            pltpu.SemaphoreType.DMA((NGRID,)),
            pltpu.SemaphoreType.DMA((BATCHES, NMIC)),
            pltpu.SemaphoreType.DMA((BATCHES, NMIC)),
        ],
        compiler_params=pltpu.CompilerParams(
            collective_id=0, has_side_effects=True, vmem_limit_bytes=32 * 1024 * 1024
        ),
    )(samples, table, mic_places, grid_places)


def solution(mesh):
    in_specs = (P("grid", "mic", None), P(None, "mic"), P(None, "grid"))
    return jax.shard_map(
        per_device, mesh=mesh, in_specs=in_specs, out_specs=P("grid"), check_vma=False
    )
```

time: 159 us -> 31.9 us (0.20)
  the two profiles are of different devices: /device:TPU:32 before, /device:TPU:1 now
where the time goes in v1:
time: 31.9 us; the launch traced here: 31.7 us
  Pallas kernels  26.6 us (83%)
  local copies, waits for them, and re-layouts  5.06 us (16%)
    pallas_call x1, Pallas kernels, per_device(): pl.pallas_call(kernel, out_shape=jax.ShapeDtypeStruct((512,), jnp.float32...  26.6 us
    unnamed x9, local copies, waits for them, and re-layouts  5.06 us

profile of v1, /device:TPU:1, one launch (start us, length us, event | category | flops | bytes accessed | tf_op | source)
XLA Modules:
  0.0 31.7 jit_solution(2191343397406592415)
XLA Ops:
  0.0 0.0 copy-start
  0.0 2.2 %copy-done = bf16[1,512,4096]{2,1,0:T(8,128)(2,1)S(1)} copy-done((bf16[1,512,4096]{2,1,0:T(8,128)(2,1)S(1)}, bf16[1,512,4096]{2,1,0:T(8,128)(2,1)}, u32[]{:S(2)}) %copy-start) | copy-done | bytes 4194328
  2.2 0.0 copy-start.1
  2.2 0.9 %copy-done.1 = bf16[16,4096]{1,0:T(8,128)(2,1)S(1)} copy-done((bf16[16,4096]{1,0:T(8,128)(2,1)S(1)}, bf16[16,4096]{1,0:T(8,128)(2,1)}, u32[]{:S(2)}) %copy-start.1) | copy-done | bytes 131096
  3.1 0.0 copy-start.2
  3.1 0.7 %copy-done.2 = f32[3,512]{1,0:T(4,128)S(1)} copy-done((f32[3,512]{1,0:T(4,128)S(1)}, f32[3,512]{1,0:T(4,128)}, u32[]{:S(2)}) %copy-start.2) | copy-done | bytes 6168
  3.8 0.0 copy-start.3
  3.8 0.7 %copy-done.3 = f32[3,512]{1,0:T(4,128)S(1)} copy-done((f32[3,512]{1,0:T(4,128)S(1)}, f32[3,512]{1,0:T(4,128)}, u32[]{:S(2)}) %copy-start.3) | copy-done | bytes 6168
  4.5 26.6 %shard_map.46 = f32[512]{0:T(512)S(1)} custom-call(bf16[1,512,4096]{2,1,0:T(8,128)(2,1)S(1)} %copy-done, bf16[16,4096]{1,0:T(8,128)(2,1)S(1)} %copy-done.1, f32[3,512]{1,0:T(4,128)S(1)} %copy-done.2, f32[3,512]{1,0:T(4,128)S(1)} %copy-done.3), custom_call_target="tpu_custom_call" | custom-call | tf_op jit(solution)/shard_map/pallas_call | solution.py:249
  31.1 0.6 %copy.6 = f32[512]{0:T(512)} copy(f32[512]{0:T(512)S(1)} %shard_map.46) | data formatting | bytes 4096
Async XLA Ops:
  0.0 2.2 %copy-start = (bf16[1,512,4096]{2,1,0:T(8,128)(2,1)S(1)}, bf16[1,512,4096]{2,1,0:T(8,128)(2,1)}, u32[]{:S(2)}) copy-start(bf16[1,512,4096]{2,1,0:T(8,128)(2,1)} %samples.1) | copy-start | bytes 12582916
  2.2 0.9 %copy-start.1 = (bf16[16,4096]{1,0:T(8,128)(2,1)S(1)}, bf16[16,4096]{1,0:T(8,128)(2,1)}, u32[]{:S(2)}) copy-start(bf16[16,4096]{1,0:T(8,128)(2,1)} %constant.2.clone.table_hbm) | copy-start | bytes 393220
  3.1 0.7 %copy-start.2 = (f32[3,512]{1,0:T(4,128)S(1)}, f32[3,512]{1,0:T(4,128)}, u32[]{:S(2)}) copy-start(f32[3,512]{1,0:T(4,128)} %mic_hbm.1) | copy-start | bytes 18436
  3.8 0.7 %copy-start.3 = (f32[3,512]{1,0:T(4,128)S(1)}, f32[3,512]{1,0:T(4,128)}, u32[]{:S(2)}) copy-start(f32[3,512]{1,0:T(4,128)} %grid_hbm.1) | copy-start | bytes 18436

commit v2 on v1

v2 whole, which is shorter than its diff:
```python
import jax
import jax.numpy as jnp
import ml_dtypes
import numpy as np
from jax import lax
from jax.experimental import pallas as pl
from jax.experimental.pallas import tpu as pltpu
from jax.sharding import PartitionSpec as P

L = 4096
BIN = 512
WAVENUMBER = 120.0
MESH = pl.DeviceIdType.MESH

NMIC = 8
NGRID = 32
NZ = 8
PARTS = 4
HALF = 4
CUBE = 16
BATCHES = ((0, 16), (0, 8), (8, 8))


def tiles_of(b):
    return BATCHES[b][1] // 2 + (b == len(BATCHES) - 1)


def dft_table():
    steps = np.arange(L, dtype=np.int64)
    window = (0.5 - 0.5 * np.cos(2.0 * np.pi * steps / L)).astype(np.float32)
    scale = np.sqrt(np.sum(window.astype(np.float64) ** 2)).astype(np.float32)
    theta = 2.0 * np.pi * ((BIN * steps) % L) / L
    cosine = np.round(np.cos(theta), 12)
    sine = np.round(np.sin(theta), 12)
    size = np.maximum(np.abs(cosine), np.abs(sine)).astype(np.float32)
    magnitude = (window * size / scale).astype(ml_dtypes.bfloat16).astype(np.float32)
    signs = [np.sign(cosine) if r < 4 else -np.sign(sine) for r in range(8)]
    return np.stack([magnitude] * 8), np.stack(signs)[:, :128].astype(np.float32)


def sine_cosine(turns):
    r = turns - jnp.round(turns)
    u = r * r
    s = SIN[-1]
    for coefficient in SIN[-2::-1]:
        s = s * u + coefficient
    s = s * r
    c = COS[-1]
    for coefficient in COS[-2::-1]:
        c = c * u + coefficient
    return s * c, 1.0 - s * s


def fitted():
    nodes = 0.125 - 0.125 * np.cos(np.pi * (np.arange(400) + 0.5) / 400)
    r = np.sqrt(nodes)
    sin_fit = np.polynomial.chebyshev.Chebyshev.fit(nodes, np.sqrt(2) * np.sin(np.pi * r) / r, 4, domain=[0, 0.25])
    cos_fit = np.polynomial.chebyshev.Chebyshev.fit(nodes, np.sqrt(2) * np.cos(np.pi * r), 4, domain=[0, 0.25])
    as_list = lambda fit: [float(v) for v in fit.convert(kind=np.polynomial.Polynomial).coef]
    return as_list(sin_fit), as_list(cos_fit)


SIN, COS = fitted()


def slot_of(grid):
    return (grid // 2 % NZ) * 4 + (grid // 16) * 2 + grid % 2


def grid_of(slot):
    return (slot // 2 % 2) * 16 + (slot // 4) * 2 + slot % 2


def kernel(
    samples, table_hbm, signs_hbm, mic_hbm, grid_hbm, out_ref,
    parts, table, signs, folded, mic, grid, mic_columns, gather, unpacked, weights, beams,
    load_sem, small_sem, gsend, grecv, bsend, brecv,
):
    me_mic = lax.axis_index("mic")
    me_grid = lax.axis_index("grid")
    me = slot_of(me_grid)
    height = 512 // PARTS

    smalls = [
        pltpu.make_async_copy(src, dst, small_sem.at[i])
        for i, (src, dst) in enumerate(
            [(table_hbm, table), (signs_hbm, signs), (mic_hbm, mic), (grid_hbm, grid)]
        )
    ]
    loads = [
        pltpu.make_async_copy(
            samples.at[0, pl.ds(p * height, height)],
            parts.at[pl.ds(p * height, height)],
            load_sem.at[p],
        )
        for p in range(PARTS)
    ]
    loads[0].start()
    smalls[0].start()
    for load in loads[1:]:
        load.start()
    for small in smalls[1:]:
        small.start()

    barrier = pltpu.get_barrier_semaphore()
    my_z = me // 4
    late = my_z // HALF
    own_base = late * CUBE

    def near(k):
        return own_base + lax.rem(me - own_base + k, CUBE)

    def across(k):
        z = jnp.where(late == 1, k // 4, NZ - 1 - k // 4)
        return z * 4 + lax.rem(me + k, 4)

    def mic_peer(k):
        return lax.rem(me_mic + k, NMIC)

    def signal(mic_index, slot):
        pl.semaphore_signal(
            barrier, inc=1, device_id=(mic_index, grid_of(slot)), device_id_type=MESH
        )

    @pl.when(late == 0)
    def _():
        for k in range(CUBE):
            signal(me_mic, across(k))

    for k in range(1, CUBE):
        signal(me_mic, near(k))
    for k in range(1, NMIC):
        signal(mic_peer(k), me)

    def spectra_copy(k, slot):
        return pltpu.make_async_remote_copy(
            src_ref=gather.at[me],
            dst_ref=gather.at[me],
            send_sem=gsend.at[k],
            recv_sem=grecv.at[me],
            device_id=(me_mic, grid_of(slot)),
            device_id_type=MESH,
        )

    def arrival(slot):
        return pltpu.make_async_remote_copy(
            src_ref=gather.at[slot],
            dst_ref=gather.at[slot],
            send_sem=gsend.at[0],
            recv_sem=grecv.at[slot],
            device_id=(me_mic, me_grid),
            device_id_type=MESH,
        )

    fold = 64

    def fold_rows(i, carry):
        at = pl.multiple_of(i * fold, fold)
        total = jnp.zeros((fold, 128), jnp.float32)
        for t in range(0, L, 128):
            factor = jnp.concatenate([table[:, t : t + 128]] * (fold // 8), axis=0)
            total += parts[pl.ds(at, fold), t : t + 128].astype(jnp.float32) * factor
        folded[pl.ds(at, fold), :] = total
        return carry

    smalls[0].wait()
    for p in range(PARTS):
        loads[p].wait()
        lax.fori_loop(p * height // fold, (p + 1) * height // fold, fold_rows, 0)
    smalls[1].wait()
    total = lax.dot_general(
        signs[...],
        folded[...],
        (((1,), (1,)), ((), ())),
        preferred_element_type=jnp.float32,
        precision=lax.Precision.HIGHEST,
    )
    lane_block = lax.rem(lax.broadcasted_iota(jnp.int32, (8, 128), 0), 4)
    own = total[:, :128]
    for k in range(1, 4):
        own = jnp.where(lane_block == k, total[:, 128 * k : 128 * (k + 1)], own)
    gather[me] = own.astype(jnp.bfloat16)

    pl.semaphore_wait(barrier, CUBE - 1 + NMIC - 1 + late * CUBE)

    @pl.when(late == 1)
    def _():
        for k in range(CUBE):
            spectra_copy(CUBE + k, across(k)).start()

    for k in range(1, CUBE):
        spectra_copy(k, near(k)).start()

    smalls[2].wait()
    smalls[3].wait()
    mic_columns[...] = jnp.concatenate(
        [mic[...], jnp.zeros((5, 512), jnp.float32)], axis=0
    ).T
    gx = grid[0:1, :]
    gy = grid[1:2, :]
    gz = grid[2:3, :] + 1.5
    step = 32

    def steer(i, carry):
        at = pl.multiple_of(i * step, step)
        dx = gx - mic_columns[pl.ds(at, step), 0:1]
        dy = gy - mic_columns[pl.ds(at, step), 1:2]
        dz = gz - mic_columns[pl.ds(at, step), 2:3]
        dist = jnp.sqrt(dx * dx + dy * dy + dz * dz)
        sine, cosine = sine_cosine(dist * (WAVENUMBER / (2.0 * np.pi)))
        weights[pl.ds(at, step), :] = cosine.astype(jnp.bfloat16)
        weights[pl.ds(pl.multiple_of(at + 512, step), step), :] = sine.astype(jnp.bfloat16)
        return carry

    lax.fori_loop(0, 512 // step, steer, 0)

    power = jnp.zeros((8, 128), jnp.float32)
    beam_copies = []
    for b, (start, segs) in enumerate(BATCHES):
        if b == 0:
            for k in range(1, CUBE):
                arrival(near(k)).wait_recv()
            first = own_base
        else:
            for k in range(start, start + segs):
                arrival(across(k)).wait_recv()
                if k == 0:
                    @pl.when(late == 0)
                    def _():
                        for i in range(CUBE):
                            spectra_copy(CUBE + i, across(i)).start()

            first = jnp.where(late == 1, start, NGRID - start - segs)
        rows = 2 * segs
        tiles = tiles_of(b)
        block = gather[pl.ds(first, segs)].astype(jnp.float32)
        power += jnp.sum(block * block, axis=0)
        unpacked[:segs] = block
        real = jnp.concatenate([unpacked[:segs, k, :] for k in range(4)], axis=1)
        imag = jnp.concatenate([unpacked[:segs, 4 + k, :] for k in range(4)], axis=1)
        left = jnp.concatenate(
            [
                jnp.concatenate([real, -imag], axis=1),
                jnp.concatenate([imag, real], axis=1),
            ],
            axis=0,
        ).astype(jnp.bfloat16)
        beam = jnp.dot(left, weights[...], preferred_element_type=jnp.float32)
        for i in range(rows // 16):
            for q in range(4):
                tile = beam[16 * i : 16 * (i + 1), 128 * q : 128 * (q + 1)]
                beams[b, me_mic, 4 * i + q] = tile.astype(jnp.bfloat16)
        if b == len(BATCHES) - 1:
            high = power.astype(jnp.bfloat16)
            low = (power - high.astype(jnp.float32)).astype(jnp.bfloat16)
            beams[b, me_mic, tiles - 1] = jnp.concatenate([high, low], axis=0)
        for k in range(1, NMIC):
            copy = pltpu.make_async_remote_copy(
                src_ref=beams.at[b, me_mic, pl.ds(0, tiles)],
                dst_ref=beams.at[b, me_mic, pl.ds(0, tiles)],
                send_sem=bsend.at[b, k],
                recv_sem=brecv.at[b, me_mic],
                device_id=(mic_peer(k), me_grid),
                device_id_type=MESH,
            )
            copy.start()
            beam_copies.append(copy)

    sums = [jnp.zeros((16, 128), jnp.float32) for _ in range(4)]
    for b, (start, segs) in enumerate(BATCHES):
        tiles = tiles_of(b)
        for j in range(NMIC):
            @pl.when(me_mic != j)
            def _():
                pltpu.make_async_remote_copy(
                    src_ref=beams.at[b, j, pl.ds(0, tiles)],
                    dst_ref=beams.at[b, j, pl.ds(0, tiles)],
                    send_sem=bsend.at[b, 0],
                    recv_sem=brecv.at[b, j],
                    device_id=(me_mic, me_grid),
                    device_id_type=MESH,
                ).wait_recv()
        for i in range(segs // 8):
            for q in range(4):
                whole = beams[b, 0, 4 * i + q].astype(jnp.float32)
                for j in range(1, NMIC):
                    whole += beams[b, j, 4 * i + q].astype(jnp.float32)
                sums[q] += whole * whole
    all_power = jnp.zeros((16, 128), jnp.float32)
    last = len(BATCHES) - 1
    for j in range(NMIC):
        all_power += beams[last, j, tiles_of(last) - 1].astype(jnp.float32)
    all_power = jnp.sum(all_power)
    for q in range(4):
        line = (jnp.sum(sums[q], axis=0) - all_power) * (1.0 / (NGRID * 512 * NMIC))
        out_ref[pl.ds(128 * q, 128)] = line

    for k in range(1, 2 * CUBE):
        spectra_copy(k, me).wait_send()
    for copy in beam_copies:
        copy.wait_send()


def per_device(samples, mic_places, grid_places):
    hbm = pl.BlockSpec(memory_space=pltpu.HBM)
    table, signs = dft_table()
    return pl.pallas_call(
        kernel,
        out_shape=pltpu.VMEM((512,), jnp.float32),
        in_specs=[hbm] * 5,
        out_specs=pl.BlockSpec(memory_space=pltpu.VMEM),
        scratch_shapes=[
            pltpu.VMEM((512, L), jnp.bfloat16),
            pltpu.VMEM((8, L), jnp.float32),
            pltpu.VMEM((8, 128), jnp.float32),
            pltpu.VMEM((512, 128), jnp.float32),
            pltpu.VMEM((3, 512), jnp.float32),
            pltpu.VMEM((3, 512), jnp.float32),
            pltpu.VMEM((512, 8), jnp.float32),
            pltpu.VMEM((NGRID, 8, 128), jnp.bfloat16),
            pltpu.VMEM((CUBE, 8, 128), jnp.float32),
            pltpu.VMEM((1024, 512), jnp.bfloat16),
            pltpu.VMEM((len(BATCHES), NMIC, 8, 16, 128), jnp.bfloat16),
            pltpu.SemaphoreType.DMA((PARTS,)),
            pltpu.SemaphoreType.DMA((4,)),
            pltpu.SemaphoreType.DMA((NGRID,)),
            pltpu.SemaphoreType.DMA((NGRID,)),
            pltpu.SemaphoreType.DMA((len(BATCHES), NMIC)),
            pltpu.SemaphoreType.DMA((len(BATCHES), NMIC)),
        ],
        compiler_params=pltpu.CompilerParams(
            collective_id=0, has_side_effects=True, vmem_limit_bytes=60 * 1024 * 1024
        ),
    )(samples, jnp.asarray(table), jnp.asarray(signs), mic_places, grid_places)


def solution(mesh):
    in_specs = (P("grid", "mic", None), P(None, "mic"), P(None, "grid"))
    return jax.shard_map(
        per_device, mesh=mesh, in_specs=in_specs, out_specs=P("grid"), check_vma=False
    )
```

time: 31.9 us -> 23.8 us (0.75)
  local copies, waits for them, and re-layouts: 5.06 us -> 0.58 us
  Pallas kernels: 26.6 us -> 23.1 us
    unnamed x9 -> x1, local copies, waits for them, and re-layouts: 5.06 us -> 0.58 us
    pallas_call x1, Pallas kernels: 26.6 us -> 23.1 us  [per_device(): pl.pallas_call(kernel, out_shape=pltpu.VMEM((512,), jnp.float32), in_spec...]
where the time goes in v2:
time: 23.8 us; the launch traced here: 23.7 us
  Pallas kernels  23.1 us (97%)
  local copies, waits for them, and re-layouts  0.58 us (2%)
    pallas_call x1, Pallas kernels, per_device(): pl.pallas_call(kernel, out_shape=pltpu.VMEM((512,), jnp.float32), in_spec...  23.1 us
    unnamed x1, local copies, waits for them, and re-layouts  0.58 us

profile of v2, /device:TPU:1, one launch (start us, length us, event | category | flops | bytes accessed | tf_op | source)
XLA Modules:
  0.0 23.7 jit_solution(696694729505557383)
XLA Ops:
  0.0 23.1 %shard_map.55 = f32[512]{0:T(512)S(1)} custom-call(bf16[1,512,4096]{2,1,0:T(8,128)(2,1)} %samples.1, f32[8,4096]{1,0:T(8,128)} %constant.4.clone.table_hbm, f32[8,128]{1,0:T(8,128)} %constant.5.clone.signs_hbm, f32[3,512]{1,0:T(4,128)} %mic_hbm.1, f32[3,512]{1,0:T(4,128)} %grid_hbm.1), custom_call_target="tpu_custom_call" | custom-call | tf_op jit(solution)/shard_map/pallas_call | solution.py:307
  23.1 0.6 %copy.7 = f32[512]{0:T(512)} copy(f32[512]{0:T(512)S(1)} %shard_map.55) | data formatting | bytes 4096

commit v3 on v2

--- a/solution.py
+++ b/solution.py
@@ -18,11 +18,11 @@
 PARTS = 4
 HALF = 4
 CUBE = 16
-BATCHES = ((0, 16), (0, 8), (8, 8))
+BATCHES = ((0, 0, 8), (0, 8, 8), (1, 0, 8), (1, 8, 8))
 
 
 def tiles_of(b):
-    return BATCHES[b][1] // 2 + (b == len(BATCHES) - 1)
+    return BATCHES[b][2] // 2 + (b == len(BATCHES) - 1)
 
 
 def dft_table():
@@ -110,12 +110,17 @@
     def near(k):
         return own_base + lax.rem(me - own_base + k, CUBE)
 
+    upwards = jnp.where(late == 1, 1, (me // 4) // 2)
+
     def across(k):
-        z = jnp.where(late == 1, k // 4, NZ - 1 - k // 4)
-        return z * 4 + lax.rem(me + k, 4)
+        z = jnp.where(upwards == 1, k // 4, HALF - 1 - k // 4)
+        return CUBE - own_base + z * 4 + lax.rem(me + k, 4)
+
+    mic_steps = [(2, 1), (2, 0), (1, 1), (3, 1), (1, 0), (3, 0), (0, 1)]
 
     def mic_peer(k):
-        return lax.rem(me_mic + k, NMIC)
+        step, other = mic_steps[k - 1]
+        return lax.rem(me_mic // 2 + step, 4) * 2 + lax.rem(me_mic + other, 2)
 
     def signal(mic_index, slot):
         pl.semaphore_signal(
@@ -214,13 +219,23 @@
 
     lax.fori_loop(0, 512 // step, steer, 0)
 
+    def tile_of(beam, t):
+        if beam.shape[0] == 8:
+            return jnp.concatenate(
+                [beam[:, 256 * t : 256 * t + 128], beam[:, 256 * t + 128 : 256 * (t + 1)]], axis=0
+            )
+        i, q = t // 4, t % 4
+        return beam[16 * i : 16 * (i + 1), 128 * q : 128 * (q + 1)]
+
     power = jnp.zeros((8, 128), jnp.float32)
     beam_copies = []
-    for b, (start, segs) in enumerate(BATCHES):
-        if b == 0:
-            for k in range(1, CUBE):
-                arrival(near(k)).wait_recv()
-            first = own_base
+    for b, (far, start, segs) in enumerate(BATCHES):
+        if not far:
+            first = own_base + start
+            for k in range(segs):
+                @pl.when(me != first + k)
+                def _():
+                    arrival(first + k).wait_recv()
         else:
             for k in range(start, start + segs):
                 arrival(across(k)).wait_recv()
@@ -230,8 +245,7 @@
                         for i in range(CUBE):
                             spectra_copy(CUBE + i, across(i)).start()
 
-            first = jnp.where(late == 1, start, NGRID - start - segs)
-        rows = 2 * segs
+            first = CUBE - own_base + jnp.where(upwards == 1, start, CUBE - start - segs)
         tiles = tiles_of(b)
         block = gather[pl.ds(first, segs)].astype(jnp.float32)
         power += jnp.sum(block * block, axis=0)
@@ -246,10 +260,8 @@
             axis=0,
         ).astype(jnp.bfloat16)
         beam = jnp.dot(left, weights[...], preferred_element_type=jnp.float32)
-        for i in range(rows // 16):
-            for q in range(4):
-                tile = beam[16 * i : 16 * (i + 1), 128 * q : 128 * (q + 1)]
-                beams[b, me_mic, 4 * i + q] = tile.astype(jnp.bfloat16)
+        for t in range(segs // 2):
+            beams[b, me_mic, t] = tile_of(beam, t).astype(jnp.bfloat16)
         if b == len(BATCHES) - 1:
             high = power.astype(jnp.bfloat16)
             low = (power - high.astype(jnp.float32)).astype(jnp.bfloat16)
@@ -266,8 +278,13 @@
             copy.start()
             beam_copies.append(copy)
 
-    sums = [jnp.zeros((16, 128), jnp.float32) for _ in range(4)]
-    for b, (start, segs) in enumerate(BATCHES):
+    for k in range(1, 2 * CUBE):
+        spectra_copy(k, me).wait_send()
+    for copy in beam_copies[: -(NMIC - 1)]:
+        copy.wait_send()
+
+    sums = [jnp.zeros((8, 128), jnp.float32) for _ in range(4)]
+    for b, (far, start, segs) in enumerate(BATCHES):
         tiles = tiles_of(b)
         for j in range(NMIC):
             @pl.when(me_mic != j)
@@ -280,12 +297,16 @@
                     device_id=(me_mic, me_grid),
                     device_id_type=MESH,
                 ).wait_recv()
-        for i in range(segs // 8):
-            for q in range(4):
-                whole = beams[b, 0, 4 * i + q].astype(jnp.float32)
-                for j in range(1, NMIC):
-                    whole += beams[b, j, 4 * i + q].astype(jnp.float32)
-                sums[q] += whole * whole
+        for t in range(segs // 2):
+            whole = beams[b, 0, t].astype(jnp.float32)
+            for j in range(1, NMIC):
+                whole += beams[b, j, t].astype(jnp.float32)
+            whole = whole * whole
+            if segs == 4:
+                sums[2 * t] += whole[:8]
+                sums[2 * t + 1] += whole[8:]
+            else:
+                sums[t % 4] += whole[:8] + whole[8:]
     all_power = jnp.zeros((16, 128), jnp.float32)
     last = len(BATCHES) - 1
     for j in range(NMIC):
@@ -295,9 +316,7 @@
         line = (jnp.sum(sums[q], axis=0) - all_power) * (1.0 / (NGRID * 512 * NMIC))
         out_ref[pl.ds(128 * q, 128)] = line
 
-    for k in range(1, 2 * CUBE):
-        spectra_copy(k, me).wait_send()
-    for copy in beam_copies:
+    for copy in beam_copies[-(NMIC - 1) :]:
         copy.wait_send()
 
 

time: 23.8 us -> 23.3 us (0.979)
  Pallas kernels: 23.1 us -> 22.6 us
    pallas_call x1, Pallas kernels: 23.1 us -> 22.6 us  [per_device(): pl.pallas_call(kernel, out_shape=pltpu.VMEM((512,), jnp.float32), in_spec...]
where the time goes in v3:
time: 23.3 us; the launch traced here: 23.2 us
  Pallas kernels  22.6 us (97%)
  local copies, waits for them, and re-layouts  0.58 us (2%)
    pallas_call x1, Pallas kernels, per_device(): pl.pallas_call(kernel, out_shape=pltpu.VMEM((512,), jnp.float32), in_spec...  22.6 us
    unnamed x1, local copies, waits for them, and re-layouts  0.58 us

profile of v3, /device:TPU:1, one launch (start us, length us, event | category | flops | bytes accessed | tf_op | source)
XLA Modules:
  0.0 23.2 jit_solution(9772548117520184648)
XLA Ops:
  0.0 22.6 %shard_map.55 = f32[512]{0:T(512)S(1)} custom-call(bf16[1,512,4096]{2,1,0:T(8,128)(2,1)} %samples.1, f32[8,4096]{1,0:T(8,128)} %constant.4.clone.table_hbm, f32[8,128]{1,0:T(8,128)} %constant.5.clone.signs_hbm, f32[3,512]{1,0:T(4,128)} %mic_hbm.1, f32[3,512]{1,0:T(4,128)} %grid_hbm.1), custom_call_target="tpu_custom_call" | custom-call | tf_op jit(solution)/shard_map/pallas_call | solution.py:326
  22.6 0.6 %copy.7 = f32[512]{0:T(512)} copy(f32[512]{0:T(512)S(1)} %shard_map.55) | data formatting | bytes 4096

commit v4 on v3

--- a/solution.py
+++ b/solution.py
@@ -112,9 +112,14 @@
 
     upwards = jnp.where(late == 1, 1, (me // 4) // 2)
 
+    spot = lax.rem(me, 4)
+
     def across(k):
         z = jnp.where(upwards == 1, k // 4, HALF - 1 - k // 4)
-        return CUBE - own_base + z * 4 + lax.rem(me + k, 4)
+        return CUBE - own_base + z * 4 + place(k % 4)
+
+    def place(k):
+        return (3 - spot, lax.rem(spot + 2, 4), spot + 1 - 2 * lax.rem(spot, 2), spot)[k]
 
     mic_steps = [(2, 1), (2, 0), (1, 1), (3, 1), (1, 0), (3, 0), (0, 1)]
 
@@ -137,25 +142,32 @@
     for k in range(1, NMIC):
         signal(mic_peer(k), me)
 
-    def spectra_copy(k, slot):
+    def spectra_copy(slot, semaphore):
         return pltpu.make_async_remote_copy(
             src_ref=gather.at[me],
             dst_ref=gather.at[me],
-            send_sem=gsend.at[k],
-            recv_sem=grecv.at[me],
+            send_sem=gsend,
+            recv_sem=grecv.at[semaphore],
             device_id=(me_mic, grid_of(slot)),
             device_id_type=MESH,
         )
 
-    def arrival(slot):
+    def spectra_wait(first, count, semaphore):
         return pltpu.make_async_remote_copy(
-            src_ref=gather.at[slot],
-            dst_ref=gather.at[slot],
-            send_sem=gsend.at[0],
-            recv_sem=grecv.at[slot],
+            src_ref=gather.at[pl.ds(first, count)],
+            dst_ref=gather.at[pl.ds(first, count)],
+            send_sem=gsend,
+            recv_sem=grecv.at[semaphore],
             device_id=(me_mic, me_grid),
             device_id_type=MESH,
         )
+
+    my_batch = me // 8
+
+    def crossing(k):
+        nearest = jnp.where(k // 4 < HALF // 2, NZ - 1, HALF)
+        first = (late == 1) & (me // 4 == nearest) & (k % 4 == 3)
+        return jnp.where(first, 4, my_batch)
 
     fold = 64
 
@@ -191,10 +203,10 @@
     @pl.when(late == 1)
     def _():
         for k in range(CUBE):
-            spectra_copy(CUBE + k, across(k)).start()
+            spectra_copy(across(k), crossing(k)).start()
 
     for k in range(1, CUBE):
-        spectra_copy(k, near(k)).start()
+        spectra_copy(near(k), my_batch).start()
 
     smalls[2].wait()
     smalls[3].wait()
@@ -227,25 +239,45 @@
         i, q = t // 4, t % 4
         return beam[16 * i : 16 * (i + 1), 128 * q : 128 * (q + 1)]
 
+    def beam_copy(b, slot, peer):
+        tiles = tiles_of(b)
+        return pltpu.make_async_remote_copy(
+            src_ref=beams.at[b, slot, pl.ds(0, tiles)],
+            dst_ref=beams.at[b, slot, pl.ds(0, tiles)],
+            send_sem=bsend.at[b],
+            recv_sem=brecv.at[b],
+            device_id=(peer, me_grid),
+            device_id_type=MESH,
+        )
+
+    def beam_wait(b):
+        return beam_copy(b, pl.ds(0, NMIC - 1), me_mic)
+
+    last = len(BATCHES) - 1
     power = jnp.zeros((8, 128), jnp.float32)
-    beam_copies = []
     for b, (far, start, segs) in enumerate(BATCHES):
-        if not far:
+        if far:
+            first = CUBE - own_base + jnp.where(upwards == 1, start, CUBE - start - segs)
+        else:
             first = own_base + start
-            for k in range(segs):
-                @pl.when(me != first + k)
-                def _():
-                    arrival(first + k).wait_recv()
-        else:
-            for k in range(start, start + segs):
-                arrival(across(k)).wait_recv()
-                if k == 0:
-                    @pl.when(late == 0)
-                    def _():
-                        for i in range(CUBE):
-                            spectra_copy(CUBE + i, across(i)).start()
-
-            first = CUBE - own_base + jnp.where(upwards == 1, start, CUBE - start - segs)
+        short = my_batch == first // 8
+        if far and start == 0:
+            @pl.when(late == 0)
+            def _():
+                spectra_wait(first, 1, 4).wait_recv()
+                for k in range(CUBE):
+                    spectra_copy(across(k), my_batch).start()
+
+            short = late == 0
+
+        @pl.when(short)
+        def _():
+            spectra_wait(first, segs - 1, first // 8).wait_recv()
+
+        @pl.when(jnp.logical_not(short))
+        def _():
+            spectra_wait(first, segs, first // 8).wait_recv()
+
         tiles = tiles_of(b)
         block = gather[pl.ds(first, segs)].astype(jnp.float32)
         power += jnp.sum(block * block, axis=0)
@@ -267,36 +299,16 @@
             low = (power - high.astype(jnp.float32)).astype(jnp.bfloat16)
             beams[b, me_mic, tiles - 1] = jnp.concatenate([high, low], axis=0)
         for k in range(1, NMIC):
-            copy = pltpu.make_async_remote_copy(
-                src_ref=beams.at[b, me_mic, pl.ds(0, tiles)],
-                dst_ref=beams.at[b, me_mic, pl.ds(0, tiles)],
-                send_sem=bsend.at[b, k],
-                recv_sem=brecv.at[b, me_mic],
-                device_id=(mic_peer(k), me_grid),
-                device_id_type=MESH,
-            )
-            copy.start()
-            beam_copies.append(copy)
-
-    for k in range(1, 2 * CUBE):
-        spectra_copy(k, me).wait_send()
-    for copy in beam_copies[: -(NMIC - 1)]:
-        copy.wait_send()
+            beam_copy(b, me_mic, mic_peer(k)).start()
+
+    spectra_wait(0, 2 * CUBE - 1, 0).wait_send()
+    for b in range(last):
+        beam_wait(b).wait_send()
 
     sums = [jnp.zeros((8, 128), jnp.float32) for _ in range(4)]
     for b, (far, start, segs) in enumerate(BATCHES):
         tiles = tiles_of(b)
-        for j in range(NMIC):
-            @pl.when(me_mic != j)
-            def _():
-                pltpu.make_async_remote_copy(
-                    src_ref=beams.at[b, j, pl.ds(0, tiles)],
-                    dst_ref=beams.at[b, j, pl.ds(0, tiles)],
-                    send_sem=bsend.at[b, 0],
-                    recv_sem=brecv.at[b, j],
-                    device_id=(me_mic, me_grid),
-                    device_id_type=MESH,
-                ).wait_recv()
+        beam_wait(b).wait_recv()
         for t in range(segs // 2):
             whole = beams[b, 0, t].astype(jnp.float32)
             for j in range(1, NMIC):
@@ -308,7 +320,6 @@
             else:
                 sums[t % 4] += whole[:8] + whole[8:]
     all_power = jnp.zeros((16, 128), jnp.float32)
-    last = len(BATCHES) - 1
     for j in range(NMIC):
         all_power += beams[last, j, tiles_of(last) - 1].astype(jnp.float32)
     all_power = jnp.sum(all_power)
@@ -316,8 +327,7 @@
         line = (jnp.sum(sums[q], axis=0) - all_power) * (1.0 / (NGRID * 512 * NMIC))
         out_ref[pl.ds(128 * q, 128)] = line
 
-    for copy in beam_copies[-(NMIC - 1) :]:
-        copy.wait_send()
+    beam_wait(last).wait_send()
 
 
 def per_device(samples, mic_places, grid_places):
@@ -342,10 +352,10 @@
             pltpu.VMEM((len(BATCHES), NMIC, 8, 16, 128), jnp.bfloat16),
             pltpu.SemaphoreType.DMA((PARTS,)),
             pltpu.SemaphoreType.DMA((4,)),
-            pltpu.SemaphoreType.DMA((NGRID,)),
-            pltpu.SemaphoreType.DMA((NGRID,)),
-            pltpu.SemaphoreType.DMA((len(BATCHES), NMIC)),
-            pltpu.SemaphoreType.DMA((len(BATCHES), NMIC)),
+            pltpu.SemaphoreType.DMA,
+            pltpu.SemaphoreType.DMA((5,)),
+            pltpu.SemaphoreType.DMA((len(BATCHES),)),
+            pltpu.SemaphoreType.DMA((len(BATCHES),)),
         ],
         compiler_params=pltpu.CompilerParams(
             collective_id=0, has_side_effects=True, vmem_limit_bytes=60 * 1024 * 1024

time: 23.3 us -> 22 us (0.944)
  Pallas kernels: 22.6 us -> 21.3 us
    pallas_call x1, Pallas kernels: 22.6 us -> 21.3 us  [per_device(): pl.pallas_call(kernel, out_shape=pltpu.VMEM((512,), jnp.float32), in_spec...]
where the time goes in v4:
time: 22 us; the launch traced here: 21.9 us
  Pallas kernels  21.3 us (97%)
  local copies, waits for them, and re-layouts  0.58 us (3%)
    pallas_call x1, Pallas kernels, per_device(): pl.pallas_call(kernel, out_shape=pltpu.VMEM((512,), jnp.float32), in_spec...  21.3 us
    unnamed x1, local copies, waits for them, and re-layouts  0.58 us

profile of v4, /device:TPU:1, one launch (start us, length us, event | category | flops | bytes accessed | tf_op | source)
XLA Modules:
  0.0 21.9 jit_solution(5959003893167202841)
XLA Ops:
  0.0 21.3 %shard_map.55 = f32[512]{0:T(512)S(1)} custom-call(bf16[1,512,4096]{2,1,0:T(8,128)(2,1)} %samples.1, f32[8,4096]{1,0:T(8,128)} %constant.4.clone.table_hbm, f32[8,128]{1,0:T(8,128)} %constant.5.clone.signs_hbm, f32[3,512]{1,0:T(4,128)} %mic_hbm.1, f32[3,512]{1,0:T(4,128)} %grid_hbm.1), custom_call_target="tpu_custom_call" | custom-call | tf_op jit(solution)/shard_map/pallas_call | solution.py:336
  21.3 0.6 %copy.7 = f32[512]{0:T(512)} copy(f32[512]{0:T(512)S(1)} %shard_map.55) | data formatting | bytes 4096

commit v5 on v4

--- a/solution.py
+++ b/solution.py
@@ -73,8 +73,8 @@
 
 def kernel(
     samples, table_hbm, signs_hbm, mic_hbm, grid_hbm, out_ref,
-    parts, table, signs, folded, mic, grid, mic_columns, gather, unpacked, weights, beams,
-    load_sem, small_sem, gsend, grecv, bsend, brecv,
+    parts, table, signs, folded, mic, grid, mic_columns, own_spectra, gather, unpacked, weights, beams,
+    load_sem, small_sem, gsend, grecv, bsend, brecv, there,
 ):
     me_mic = lax.axis_index("mic")
     me_grid = lax.axis_index("grid")
@@ -144,7 +144,7 @@
 
     def spectra_copy(slot, semaphore):
         return pltpu.make_async_remote_copy(
-            src_ref=gather.at[me],
+            src_ref=own_spectra,
             dst_ref=gather.at[me],
             send_sem=gsend,
             recv_sem=grecv.at[semaphore],
@@ -163,11 +163,6 @@
         )
 
     my_batch = me // 8
-
-    def crossing(k):
-        nearest = jnp.where(k // 4 < HALF // 2, NZ - 1, HALF)
-        first = (late == 1) & (me // 4 == nearest) & (k % 4 == 3)
-        return jnp.where(first, 4, my_batch)
 
     fold = 64
 
@@ -196,14 +191,21 @@
     own = total[:, :128]
     for k in range(1, 4):
         own = jnp.where(lane_block == k, total[:, 128 * k : 128 * (k + 1)], own)
-    gather[me] = own.astype(jnp.bfloat16)
+    own_spectra[...] = own.astype(jnp.bfloat16)
+    pltpu.make_async_copy(own_spectra, gather.at[me], grecv.at[my_batch]).start()
 
     pl.semaphore_wait(barrier, CUBE - 1 + NMIC - 1 + late * CUBE)
 
     @pl.when(late == 1)
     def _():
         for k in range(CUBE):
-            spectra_copy(across(k), crossing(k)).start()
+            spectra_copy(across(k), my_batch).start()
+        for z in range(HALF):
+            @pl.when(me // 4 == (NZ - 1 if z < HALF // 2 else HALF))
+            def _():
+                pl.semaphore_signal(
+                    there, inc=1, device_id=(me_mic, grid_of(z * 4 + spot)), device_id_type=MESH
+                )
 
     for k in range(1, CUBE):
         spectra_copy(near(k), my_batch).start()
@@ -260,24 +262,14 @@
             first = CUBE - own_base + jnp.where(upwards == 1, start, CUBE - start - segs)
         else:
             first = own_base + start
-        short = my_batch == first // 8
         if far and start == 0:
             @pl.when(late == 0)
             def _():
-                spectra_wait(first, 1, 4).wait_recv()
+                pl.semaphore_wait(there, 1)
                 for k in range(CUBE):
                     spectra_copy(across(k), my_batch).start()
 
-            short = late == 0
-
-        @pl.when(short)
-        def _():
-            spectra_wait(first, segs - 1, first // 8).wait_recv()
-
-        @pl.when(jnp.logical_not(short))
-        def _():
-            spectra_wait(first, segs, first // 8).wait_recv()
-
+        spectra_wait(first, segs, first // 8).wait_recv()
         tiles = tiles_of(b)
         block = gather[pl.ds(first, segs)].astype(jnp.float32)
         power += jnp.sum(block * block, axis=0)
@@ -298,8 +290,8 @@
             high = power.astype(jnp.bfloat16)
             low = (power - high.astype(jnp.float32)).astype(jnp.bfloat16)
             beams[b, me_mic, tiles - 1] = jnp.concatenate([high, low], axis=0)
-        for k in range(1, NMIC):
-            beam_copy(b, me_mic, mic_peer(k)).start()
+        for k in range(NMIC - 1):
+            beam_copy(b, me_mic, jnp.where(me_mic <= k, k + 1, k)).start()
 
     spectra_wait(0, 2 * CUBE - 1, 0).wait_send()
     for b in range(last):
@@ -308,6 +300,8 @@
     sums = [jnp.zeros((8, 128), jnp.float32) for _ in range(4)]
     for b, (far, start, segs) in enumerate(BATCHES):
         tiles = tiles_of(b)
+        if b == last:
+            beam_wait(b).wait_send()
         beam_wait(b).wait_recv()
         for t in range(segs // 2):
             whole = beams[b, 0, t].astype(jnp.float32)
@@ -327,8 +321,6 @@
         line = (jnp.sum(sums[q], axis=0) - all_power) * (1.0 / (NGRID * 512 * NMIC))
         out_ref[pl.ds(128 * q, 128)] = line
 
-    beam_wait(last).wait_send()
-
 
 def per_device(samples, mic_places, grid_places):
     hbm = pl.BlockSpec(memory_space=pltpu.HBM)
@@ -346,6 +338,7 @@
             pltpu.VMEM((3, 512), jnp.float32),
             pltpu.VMEM((3, 512), jnp.float32),
             pltpu.VMEM((512, 8), jnp.float32),
+            pltpu.VMEM((8, 128), jnp.bfloat16),
             pltpu.VMEM((NGRID, 8, 128), jnp.bfloat16),
             pltpu.VMEM((CUBE, 8, 128), jnp.float32),
             pltpu.VMEM((1024, 512), jnp.bfloat16),
@@ -353,9 +346,10 @@
             pltpu.SemaphoreType.DMA((PARTS,)),
             pltpu.SemaphoreType.DMA((4,)),
             pltpu.SemaphoreType.DMA,
-            pltpu.SemaphoreType.DMA((5,)),
+            pltpu.SemaphoreType.DMA((4,)),
             pltpu.SemaphoreType.DMA((len(BATCHES),)),
             pltpu.SemaphoreType.DMA((len(BATCHES),)),
+            pltpu.SemaphoreType.REGULAR,
         ],
         compiler_params=pltpu.CompilerParams(
             collective_id=0, has_side_effects=True, vmem_limit_bytes=60 * 1024 * 1024

time: 22 us -> 21.4 us (0.973)
  Pallas kernels: 21.3 us -> 20.7 us
    pallas_call x1, Pallas kernels: 21.3 us -> 20.7 us  [per_device(): pl.pallas_call(kernel, out_shape=pltpu.VMEM((512,), jnp.float32), in_spec...]
where the time goes in v5:
time: 21.4 us; the launch traced here: 21.3 us
  Pallas kernels  20.7 us (97%)
  local copies, waits for them, and re-layouts  0.58 us (3%)
    pallas_call x1, Pallas kernels, per_device(): pl.pallas_call(kernel, out_shape=pltpu.VMEM((512,), jnp.float32), in_spec...  20.7 us
    unnamed x1, local copies, waits for them, and re-layouts  0.58 us

profile of v5, /device:TPU:1, one launch (start us, length us, event | category | flops | bytes accessed | tf_op | source)
XLA Modules:
  0.0 21.3 jit_solution(12550298845018551902)
XLA Ops:
  0.0 20.7 %shard_map.55 = f32[512]{0:T(512)S(1)} custom-call(bf16[1,512,4096]{2,1,0:T(8,128)(2,1)} %samples.1, f32[8,4096]{1,0:T(8,128)} %constant.4.clone.table_hbm, f32[8,128]{1,0:T(8,128)} %constant.5.clone.signs_hbm, f32[3,512]{1,0:T(4,128)} %mic_hbm.1, f32[3,512]{1,0:T(4,128)} %grid_hbm.1), custom_call_target="tpu_custom_call" | custom-call | tf_op jit(solution)/shard_map/pallas_call | solution.py:328
  20.7 0.6 %copy.7 = f32[512]{0:T(512)} copy(f32[512]{0:T(512)S(1)} %shard_map.55) | data formatting | bytes 4096

commit v6 on v5

--- a/solution.py
+++ b/solution.py
@@ -164,7 +164,7 @@
 
     my_batch = me // 8
 
-    fold = 64
+    fold = 128
 
     def fold_rows(i, carry):
         at = pl.multiple_of(i * fold, fold)
@@ -287,11 +287,15 @@
         for t in range(segs // 2):
             beams[b, me_mic, t] = tile_of(beam, t).astype(jnp.bfloat16)
         if b == len(BATCHES) - 1:
-            high = power.astype(jnp.bfloat16)
-            low = (power - high.astype(jnp.float32)).astype(jnp.bfloat16)
+            whole = jnp.full((8, 128), jnp.sum(power))
+            high = whole.astype(jnp.bfloat16)
+            low = (whole - high.astype(jnp.float32)).astype(jnp.bfloat16)
             beams[b, me_mic, tiles - 1] = jnp.concatenate([high, low], axis=0)
-        for k in range(NMIC - 1):
+        def send(k, carry, b=b):
             beam_copy(b, me_mic, jnp.where(me_mic <= k, k + 1, k)).start()
+            return carry
+
+        lax.fori_loop(0, NMIC - 1, send, 0)
 
     spectra_wait(0, 2 * CUBE - 1, 0).wait_send()
     for b in range(last):
@@ -316,7 +320,7 @@
     all_power = jnp.zeros((16, 128), jnp.float32)
     for j in range(NMIC):
         all_power += beams[last, j, tiles_of(last) - 1].astype(jnp.float32)
-    all_power = jnp.sum(all_power)
+    all_power = all_power[0] + all_power[8]
     for q in range(4):
         line = (jnp.sum(sums[q], axis=0) - all_power) * (1.0 / (NGRID * 512 * NMIC))
         out_ref[pl.ds(128 * q, 128)] = line

time: 21.4 us -> 21.3 us (level)
  no operation moved by 1% of the time
where the time goes in v6:
time: 21.3 us; the launch traced here: 21.2 us
  Pallas kernels  20.6 us (97%)
  local copies, waits for them, and re-layouts  0.58 us (3%)
    pallas_call x1, Pallas kernels, per_device(): pl.pallas_call(kernel, out_shape=pltpu.VMEM((512,), jnp.float32), in_spec...  20.6 us
    unnamed x1, local copies, waits for them, and re-layouts  0.58 us

profile of v6, /device:TPU:1, one launch (start us, length us, event | category | flops | bytes accessed | tf_op | source)
XLA Modules:
  0.0 21.2 jit_solution(11948765995414159558)
XLA Ops:
  0.0 20.6 %shard_map.55 = f32[512]{0:T(512)S(1)} custom-call(bf16[1,512,4096]{2,1,0:T(8,128)(2,1)} %samples.1, f32[8,4096]{1,0:T(8,128)} %constant.4.clone.table_hbm, f32[8,128]{1,0:T(8,128)} %constant.5.clone.signs_hbm, f32[3,512]{1,0:T(4,128)} %mic_hbm.1, f32[3,512]{1,0:T(4,128)} %grid_hbm.1), custom_call_target="tpu_custom_call" | custom-call | tf_op jit(solution)/shard_map/pallas_call | solution.py:332
  20.6 0.6 %copy.7 = f32[512]{0:T(512)} copy(f32[512]{0:T(512)S(1)} %shard_map.55) | data formatting | bytes 4096

commit v7 on v6

--- a/solution.py
+++ b/solution.py
@@ -292,7 +292,9 @@
             low = (whole - high.astype(jnp.float32)).astype(jnp.bfloat16)
             beams[b, me_mic, tiles - 1] = jnp.concatenate([high, low], axis=0)
         def send(k, carry, b=b):
-            beam_copy(b, me_mic, jnp.where(me_mic <= k, k + 1, k)).start()
+            at = lax.rem(me_mic, 2) * 4 + me_mic // 2
+            u = jnp.where(at <= k, k + 1, k)
+            beam_copy(b, me_mic, lax.rem(u, 4) * 2 + u // 4).start()
             return carry
 
         lax.fori_loop(0, NMIC - 1, send, 0)
@@ -322,14 +324,14 @@
         all_power += beams[last, j, tiles_of(last) - 1].astype(jnp.float32)
     all_power = all_power[0] + all_power[8]
     for q in range(4):
-        line = (jnp.sum(sums[q], axis=0) - all_power) * (1.0 / (NGRID * 512 * NMIC))
+        line = jnp.sum(sums[q], axis=0) - all_power
         out_ref[pl.ds(128 * q, 128)] = line
 
 
 def per_device(samples, mic_places, grid_places):
     hbm = pl.BlockSpec(memory_space=pltpu.HBM)
     table, signs = dft_table()
-    return pl.pallas_call(
+    beam_map = pl.pallas_call(
         kernel,
         out_shape=pltpu.VMEM((512,), jnp.float32),
         in_specs=[hbm] * 5,
@@ -359,6 +361,7 @@
             collective_id=0, has_side_effects=True, vmem_limit_bytes=60 * 1024 * 1024
         ),
     )(samples, jnp.asarray(table), jnp.asarray(signs), mic_places, grid_places)
+    return beam_map * (1.0 / (NGRID * 512 * NMIC))
 
 
 def solution(mesh):

time: 21.3 us -> 21.4 us (level)
  other arithmetic: 0 us -> 0.58 us
  local copies, waits for them, and re-layouts: 0.58 us -> 0 us
    mul x0 -> x1, other arithmetic: none -> 0.58 us  [per_device(): return beam_map * (1.0 / (NGRID * 512 * NMIC))]
    unnamed x1 -> x0, local copies, waits for them, and re-layouts: 0.58 us -> none
where the time goes in v7:
time: 21.4 us; the launch traced here: 21.2 us
  Pallas kernels  20.6 us (96%)
  other arithmetic  0.58 us (3%)
    pallas_call x1, Pallas kernels, per_device(): pl.pallas_call(kernel, out_shape=pltpu.VMEM((512,), jnp.float32), in_spec...  20.6 us
    mul x1, other arithmetic, per_device(): return beam_map * (1.0 / (NGRID * 512 * NMIC))  0.58 us

profile of v7, /device:TPU:1, one launch (start us, length us, event | category | flops | bytes accessed | tf_op | source)
XLA Modules:
  0.0 21.2 jit_solution(8776242092434283958)
XLA Ops:
  0.0 20.6 %shard_map.55 = f32[512]{0:T(512)S(1)} custom-call(bf16[1,512,4096]{2,1,0:T(8,128)(2,1)} %samples.1, f32[8,4096]{1,0:T(8,128)} %constant.6.clone.table_hbm, f32[8,128]{1,0:T(8,128)} %constant.7.clone.signs_hbm, f32[3,512]{1,0:T(4,128)} %mic_hbm.1, f32[3,512]{1,0:T(4,128)} %grid_hbm.1), custom_call_target="tpu_custom_call" | custom-call | tf_op jit(solution)/shard_map/pallas_call | solution.py:334
  20.6 0.6 %broadcast_multiply_fusion = f32[512]{0:T(512)} fusion(f32[512]{0:T(512)S(1)} %shard_map.55), kind=kLoop, calls=%fused_computation | loop fusion | flops 512 | bytes 4096 | tf_op jit(solution)/shard_map/mul | solution.py:364
